TPU v7x, 256 devices: a whole 4x4x8 slice. The times are simulated.
256 devices in a mesh: seq: 32 (over y, z), head: 8 (over x, core).
Axes of the slice: x: 4, y: 4, z: 8, core: 2. Of those that a mesh axis runs over, the one named last changes fastest.
Arguments:
- query_act: bfloat16 [32768, 8192], P('seq', 'head'), may hold values from -6 to 6
- key_act: bfloat16 [32768, 8192], P('seq', 'head'), may hold values from -6 to 6
- value_act: bfloat16 [32768, 8192], P('seq', 'head'), may hold values from -170 to 170
- norm_gain: bfloat16 [8192], P('head'), may hold values from 0.099609375 to 1.8984375
- doc_lengths: int32 [64], replicated, may hold values from 1 to 8192, 32768 in all
Outputs:
- attended: bfloat16 [32768, 8192], P('seq', 'head')
All inputs are finite; a program needn't handle non-finite values.
Results may differ from a plain program's by a relative error of at most 0.0043.
Values sent between devices are 32-bit elements; how exact they have to be, the bound alone decides.
A program may use at most 128 MiB of HBM per device.

v0:
```python
import jax
import jax.numpy as jnp
from jax import lax
from jax.sharding import PartitionSpec as P

HEADS = 64
E = 128


def entering(part, axis, combine, identity):
    place = lax.axis_index(axis)
    gathered = jax.tree.map(lambda a: lax.all_gather(a, axis), part)
    state = jax.tree.map(lambda a, e: jnp.zeros_like(a) + jnp.asarray(e, a.dtype), part, identity)

    def one(step, state):
        return combine(
            state, jax.tree.map(lambda a: lax.dynamic_index_in_dim(a, step, 0, False), gathered)
        )

    return lax.fori_loop(0, place, one, state)


def feature_map(inputs):
    return (jax.nn.elu(inputs.astype(jnp.float32)) + 1.0).astype(jnp.bfloat16)


def doc_index(positions, doc_lengths):
    doc_ends = jnp.cumsum(doc_lengths, dtype=jnp.int32)
    return jnp.sum(
        (doc_ends[None, :] <= positions[:, None]).astype(jnp.int32), axis=1, dtype=jnp.int32
    )


def block_pair(query_rows, key_rows, value_rows, query_docs, key_docs, diagonal):
    scores = jnp.einsum("qhe,khe->hqk", query_rows, key_rows, preferred_element_type=jnp.float32)
    retain = query_docs[:, None] == key_docs[None, :]
    if diagonal:
        offsets = jnp.arange(query_rows.shape[0], dtype=jnp.int32)
        retain = retain & (offsets[:, None] >= offsets[None, :])
    masked_scores = jnp.where(retain[None], scores, 0.0)
    denominator = jnp.sum(masked_scores, axis=2).T
    weights = masked_scores.astype(jnp.bfloat16)
    numerator = jnp.einsum("hqk,khe->qhe", weights, value_rows, preferred_element_type=jnp.float32)
    return (numerator, denominator)


def body(query_act, key_act, value_act, norm_gain, doc_lengths):
    row_count = query_act.shape[0]
    feat_width = query_act.shape[1]
    head_count = feat_width // E
    shard_id = lax.axis_index("seq")
    positions = shard_id * row_count + jnp.arange(row_count, dtype=jnp.int32)
    doc_ids = doc_index(positions, doc_lengths)
    query_feats = feature_map(query_act).reshape(row_count, head_count, E)
    key_feats = feature_map(key_act).reshape(row_count, head_count, E)
    value_per_head = value_act.reshape(row_count, head_count, E)
    block_rows = min(512, row_count)
    block_count = row_count // block_rows
    num_parts = []
    den_parts = []
    for q_block in range(block_count):
        q_slice = slice(q_block * block_rows, (q_block + 1) * block_rows)
        numerator = jnp.zeros((block_rows, head_count, E), jnp.float32)
        denominator = jnp.zeros((block_rows, head_count), jnp.float32)
        for k_block in range(q_block + 1):
            k_slice = slice(k_block * block_rows, (k_block + 1) * block_rows)
            if k_block < q_block:
                pair_num, pair_den = block_pair(
                    query_feats[q_slice],
                    key_feats[k_slice],
                    value_per_head[k_slice],
                    doc_ids[q_slice],
                    doc_ids[k_slice],
                    False,
                )
            else:
                pair_num, pair_den = block_pair(
                    query_feats[q_slice],
                    key_feats[k_slice],
                    value_per_head[k_slice],
                    doc_ids[q_slice],
                    doc_ids[k_slice],
                    True,
                )
            numerator = numerator + pair_num
            denominator = denominator + pair_den
        num_parts.append(numerator)
        den_parts.append(denominator)
    local_num = jnp.concatenate(num_parts, axis=0)
    local_den = jnp.concatenate(den_parts, axis=0)
    trailing_keys = jnp.where(
        (doc_ids == doc_ids[row_count - 1])[:, None, None], key_feats, jnp.zeros_like(key_feats)
    )
    trailing_state = jnp.einsum(
        "uzb,uzi->zbi", trailing_keys, value_per_head, preferred_element_type=jnp.float32
    )
    tail_norm = jnp.sum(trailing_keys, axis=0, dtype=jnp.float32)
    prev_last = doc_index(jnp.reshape(shard_id * row_count - 1, (1,)), doc_lengths)[0]
    starts = (doc_ids[row_count - 1] != prev_last).astype(jnp.float32).reshape(1)

    def combine(earlier, following):
        keep_old = 1.0 - following[0][0]
        return (
            jnp.maximum(earlier[0], following[0]),
            following[1] + keep_old * earlier[1],
            following[2] + keep_old * earlier[2],
        )

    identity = (
        jnp.zeros((1,), jnp.float32),
        jnp.zeros_like(trailing_state),
        jnp.zeros_like(tail_norm),
    )
    leading_part = entering((starts, trailing_state, tail_norm), "seq", combine, identity)
    follow = ((doc_ids[0] == prev_last) & (shard_id > 0)).astype(jnp.float32)
    carried_state = follow * leading_part[1]
    carried_norm = follow * leading_part[2]
    query_wide = query_feats.astype(jnp.float32)
    carry_num = jnp.einsum(
        "qhe,hef->qhf", query_wide, carried_state, precision=lax.Precision.HIGHEST
    )
    carry_den = jnp.einsum("qhe,he->qh", query_wide, carried_norm, precision=lax.Precision.HIGHEST)
    inside_first_document = doc_ids == doc_ids[0]
    numerator_all = local_num + jnp.where(inside_first_document[:, None, None], carry_num, 0.0)
    denominator_all = local_den + jnp.where(inside_first_document[:, None], carry_den, 0.0)
    attention = numerator_all / denominator_all[:, :, None]
    flattened = attention.reshape(row_count, feat_width)
    square_part = jnp.sum(flattened * flattened, axis=1)
    square_total = lax.psum(square_part, "head")
    mean_square = square_total / (HEADS * E)
    scaled = (
        flattened * lax.rsqrt(mean_square + 1e-06)[:, None] * norm_gain.astype(jnp.float32)[None, :]
    )
    return scaled.astype(jnp.bfloat16)


def solution(mesh):
    in_specs = (P("seq", "head"), P("seq", "head"), P("seq", "head"), P("head"), P())
    out_specs = P("seq", "head")
    return jax.shard_map(body, mesh=mesh, in_specs=in_specs, out_specs=out_specs, check_vma=False)
```

profile of v0, /device:TPU:249, one launch (start us, length us, event | category | flops | bytes accessed | tf_op | source)
XLA Modules:
  0.0 298.3 jit_solution(6095715821614579233)
XLA Ops:
  8.7 3.9 %copy.63 = bf16[1024,1024]{0,1:T(8,128)(2,1)} copy(bf16[1024,1024]{1,0:T(8,128)(2,1)} %param.8) | data formatting | bytes 4194304 | tf_op args[1]
  14.1 4.0 %convert_reduce_fusion = (f32[1024]{0:T(1024)S(1)}, bf16[1024,1024]{0,1:T(8,128)(2,1)S(1)}) fusion(pred[1024]{0:T(1024)(128)(4,1)S(1)} %get-tuple-element.91, bf16[1024,1024]{0,1:T(8,128)(2,1)} %copy.63), kind=kLoop, calls=%fused_computation.28 | loop fusion | flops 9436160 | bytes 4199424 | tf_op jit(solution)/shard_map/reduce_sum | solution.py:97
  22.3 3.9 %copy.62 = bf16[1024,1024]{0,1:T(8,128)(2,1)} copy(bf16[1024,1024]{1,0:T(8,128)(2,1)} %param.7) | data formatting | bytes 4194304 | tf_op args[0]
  26.2 2.7 fusion.37
  28.9 2.3 copy.102
  34.0 56.1 %all-reduce = f32[32]{0:T(128)S(1)} all-reduce(f32[32]{0:T(128)S(1)} %dynamic-update-slice), channel_id=1, replica_groups=mesh['seq'=32,'head'=8] {'seq'}, use_global_device_ids=true, to_apply=%add | all-reduce | flops 32 | bytes 256
  90.1 38.7 %all_gather.19 = f32[32,8,128]{2,1,0:T(8,128)S(1)} all-gather(f32[1,8,128]{2,1,0:T(8,128)S(1)} %bitcast.85), channel_id=1, replica_groups=mesh['seq'=32,'head'=8] {'seq'}, dimensions={0}, use_global_device_ids=true | all-gather | bytes 135168 | tf_op jit(solution)/shard_map/all_gather | solution.py:12
  129.5 1.9 fusion.5
  135.9 3.1 %fusion.23 = f32[512,8,128]{2,0,1:T(8,128)} fusion(bf16[512,8,128]{0,2,1:T(8,128)(2,1)S(1)} %bitcast.74, bf16[8,512,512]{1,2,0:T(8,128)(2,1)S(1)} %get-tuple-element.104, pred[512,512]{0,1:T(8,128)(4,1)S(1)} %get-tuple-element.96), kind=kOutput, calls=%fused_computation.41 | convolution fusion | flops 538968064 | bytes 7602176 | tf_op jit(solution)/shard_map/hqk,khe->qhe/dot_general | solution.py:43
  140.8 3.4 %add_bitcast_fusion = f32[512,8,128]{2,0,1:T(8,128)} fusion(f32[8,512,128]{2,1,0:T(8,128)S(1)} %fusion.1, bf16[512,8,128]{0,2,1:T(8,128)(2,1)S(1)} %bitcast.73, bf16[8,512,512]{1,2,0:T(8,128)(2,1)S(1)} %get-tuple-element.102, pred[512,512]{0,1:T(8,128)(4,1)S(1)} %get-tuple-element.98), kind=kOutput, calls=%fused_computation.39 | convolution fusion | flops 539492352 | bytes 9699328 | tf_op jit(solution)/shard_map/hqk,khe->qhe/dot_general | solution.py:43
  144.3 13.1 %all-gather.3.cloned.1.call-done = f32[256,128,128]{2,1,0:T(8,128)} async-done(((f32[8,128,128]{2,1,0:T(8,128)}), f32[256,128,128]{2,1,0:T(8,128)}) %all-gather.3.cloned.1.call-update) | async-done | bytes 16777232 | tf_op jit(solution)/shard_map/all_gather | solution.py:12
  157.4 96.6 %while.14 = (s32[]{:T(128)}, f32[8,128,128]{2,1,0:T(8,128)S(1)}, f32[8,128]{1,0:T(8,128)S(1)}, s32[]{:T(128)}, f32[32,8,128,128]{3,2,1,0:T(8,128)}, /*index=5*/f...) while((s32[]{:T(128)}, f32[8,128,128]{2,1,0:T(8,128)S(1)}, ...), condition=%wide.region_5.6_spmd, body=%wide.region_4.5_spmd.sunk | while | flops 264198 | bytes 1585323 | solution.py:20
  158.7 1.9 bitcast_add_fusion.4
  161.8 1.9 bitcast_add_fusion.4
  164.9 1.9 bitcast_add_fusion.4
  168.0 1.9 bitcast_add_fusion.4
  180.5 1.9 bitcast_add_fusion.4
  183.6 1.9 bitcast_add_fusion.4
  186.7 1.9 bitcast_add_fusion.4
  254.9 7.8 %multiply_reduce_fusion = (f32[1024]{0:T(1024)S(1)}, f32[1024,8,128]{2,0,1:T(8,128)}) fusion(f32[1024,8]{0,1:T(8,128)S(1)} %maximum_add_fusion.1, bf16[1024,8,128]{0,2,1:T(8,128)(2,1)S(1)} %bitcast.71, f32[8,128,128]{2,1,0:T(8,128)S(1)} %get-tuple-element.64, f32[]{:T(128)S(6)} %convert_element_type.60, pred[1024]{0:T(1024)(128)(4,1)S(1)} %get-tuple-element.90, ...), kind=kOutput, calls=%fused_computation.27 | convolution fusion | flops 1617034240 | bytes 11047940 | tf_op jit(solution)/shard_map/qhe,hef->qhf/dot_general | solution.py:119
  262.8 18.2 %psum.7 = f32[1024]{0:T(1024)S(1)} all-reduce(f32[1024]{0:T(1024)S(1)} %get-tuple-element.105), channel_id=1, replica_groups=mesh['seq'=32,'head'=8] {'head'}, use_global_device_ids=true, to_apply=%region_10.11 | all-reduce | flops 1024 | bytes 8192 | tf_op jit(solution)/shard_map/psum | solution.py:129
  280.9 5.3 %copy.82 = f32[1024,8,128]{0,2,1:T(8,128)} copy(f32[1024,8,128]{2,0,1:T(8,128)} %get-tuple-element.106) | data formatting | bytes 8388608 | tf_op jit(solution)/shard_map/div | solution.py:126
  286.3 2.6 fusion.11
  288.9 2.6 copy.83
  (128 shorter events, 98.7 us)
Async XLA Ops:
  6.5 150.8 %all-gather.3.cloned.1.call-start = ((), (), s32[]{:S(2)}) async-start(), calls=%async_computation | async-start | bytes 17301504 | tf_op jit(solution)/shard_map/all_gather | solution.py:12
  12.7 5.5 %copy-start.1 = (bf16[1024,1024]{1,0:T(8,128)(2,1)S(1)}, bf16[1024,1024]{1,0:T(8,128)(2,1)}, u32[]{:S(2)}) copy-start(bf16[1024,1024]{1,0:T(8,128)(2,1)} %param.9) | copy-start | bytes 6291460
  18.2 4.1 %copy-start.4 = (bf16[1024]{0:T(1024)(128)(2,1)S(1)}, bf16[1024]{0:T(1024)(128)(2,1)}, u32[]{:S(2)}) copy-start(bf16[1024]{0:T(1024)(128)(2,1)} %param.10) | copy-start | bytes 6148
  26.2 6.4 %copy-start.5 = (u32[256]{0:T(256)S(1)}, u32[256]{0:T(256)}, u32[]{:S(2)}) copy-start(u32[256]{0:T(256)} %constant.62) | copy-start | bytes 3076
  90.1 39.3 %copy-start = (bf16[1024,1024]{0,1:T(8,128)(2,1)S(1)}, bf16[1024,1024]{0,1:T(8,128)(2,1)}, u32[]{:S(2)}) copy-start(bf16[1024,1024]{0,1:T(8,128)(2,1)} %copy.62) | copy-start | bytes 6291460
  134.4 1.5 copy-start.3
  139.1 1.8 copy-start.2
Sparse Core Ops, SparseCore 0:
  19.9 137.3 all-gather.2
where the time goes:
time: 301 us; the launch traced here: 298 us
  blocking collectives  113 us (38%)
  other arithmetic  107 us (36%)
  local copies, waits for them, and re-layouts  25.3 us (8%)
  matrix products  23 us (8%)
  between operations  16 us (5%)
  waiting for transfers between devices  13.1 us (4%)
    add x31, other arithmetic, combine(): following[1] + keep_old * earlier[1]  57.4 us
    unnamed x1, blocking collectives  56.1 us
    all_gather x1, blocking collectives, entering(): gathered = jax.tree.map(lambda a: lax.all_gather(a, axis), part)  38.7 us
    sub x31, other arithmetic, combine(): keep_old = 1.0 - following[0][0]  19.2 us
    add x31, other arithmetic, combine(): following[2] + keep_old * earlier[2]  19.1 us
    psum x1, blocking collectives, body(): square_total = lax.psum(square_part, 'head')  18.2 us
    all_gather x1, waiting for transfers between devices, entering(): gathered = jax.tree.map(lambda a: lax.all_gather(a, axis), part)  13.1 us
    unnamed x19, local copies, waits for them, and re-layouts  13 us
  transfers between devices with their start and end apart: 1, of which 1 were waited for; matrix products, arithmetic and copies ran while one was open for 9% of the time, Pallas kernels for 0%

commit v1 on v0

v1 whole, which is shorter than its diff:
```python
import functools

import jax
import jax.numpy as jnp
from jax import lax
from jax.experimental import pallas as pl
from jax.experimental.pallas import tpu as pltpu
from jax.sharding import PartitionSpec as P

E = 128
ROWS = 136
MESH = pl.DeviceIdType.MESH
F32 = jnp.float32
BF16 = jnp.bfloat16
H1_SLOT, H2_SLOT, H3_SLOT = 0, 3, 6


def feature_map(x):
    x = x.astype(F32)
    return jnp.where(x > 0.0, x + 1.0, jnp.exp(x)).astype(BF16)


def kernel(
    n_seq, n_head, n_feat,
    q_hbm, k_hbm, v_hbm, len_ref,
    att_hbm, scale_ref,
    qraw, kraw, vraw, qf, kft, tails, nd, att, sqacc,
    mask, cmask, tmask, dl, df,
    wr, sr, yr, tr, wo, so, tm, sq,
    in_sem, out_sem,
    wr_s, wr_r, sr_s, sr_r, yr_s, yr_r, tr_s, tr_r, sq_s, sq_r,
):
    heads, tok, _ = qraw.shape
    groups = tok // 128
    i = lax.axis_index("seq")
    hd = lax.axis_index("head")

    def shard(d):
        return (lax.rem(i + d + n_seq, n_seq), hd)

    def peer(j):
        return (i, lax.rem(hd + j, n_head))

    def position(j):
        return jnp.where(j < 4, 3 * lax.rem(j, 2), 1 + lax.rem(j, 2))

    def head_of(p, u):
        return lax.rem(i - p + 4 * n_seq, 4) + 4 * u

    def col(ref, h):
        return ref.at[:, pl.ds(pl.multiple_of(h * E, E), E)]

    def load(which, h):
        src, dst = ((q_hbm, qraw), (k_hbm, kraw), (v_hbm, vraw))[which]
        return pltpu.make_async_copy(col(src, h), dst.at[h], in_sem.at[which, h])

    barrier = pltpu.get_barrier_semaphore()
    senders = [shard(d) for d in (-1, 1, -8, -3, -5, -7)]
    senders += [peer(j) for j in range(1, n_head)]
    for dev in senders:
        pl.semaphore_signal(barrier, inc=1, device_id=dev, device_id_type=MESH)

    @pl.loop(0, heads)
    def _(j):
        h = head_of(position(j), lax.rem(j // 2, 2))
        load(1, h).start()
        load(2, h).start()

    @pl.loop(0, heads)
    def _(h):
        load(0, h).start()

    base = i * tok
    lane8 = lax.broadcasted_iota(jnp.int32, (8, 128), 1)
    sub8 = lax.broadcasted_iota(jnp.int32, (8, 128), 0)
    sub16 = lax.broadcasted_iota(jnp.int32, (16, 128), 0)
    pos_tok = base + sub8 * 128 + lane8
    pos_last = (i - 7 + sub16) * tok - 1
    pos_first = jnp.zeros((8, 128), jnp.int32) + base
    st_tok = jnp.zeros((8, 128), jnp.int32)
    st_last = jnp.where(pos_last < 0, -1, 0)
    st_first = jnp.zeros((8, 128), jnp.int32)
    end = jnp.int32(0)
    for d in range(len_ref.shape[0]):
        end = end + len_ref[d]
        st_tok = jnp.where(pos_tok >= end, end, st_tok)
        st_last = jnp.where(pos_last >= end, end, st_last)
        st_first = jnp.where(pos_first >= end, end, st_first)
    dl[...] = st_last
    df[...] = st_first

    lane = lax.broadcasted_iota(jnp.int32, (128, 128), 1).astype(F32)
    sub = lax.broadcasted_iota(jnp.int32, (128, 128), 0).astype(F32)
    st_loc = (st_tok - base).astype(F32)
    tail_start = (st_last[8:9, :] - base).astype(F32)
    one, zero = jnp.ones((128, 128), F32), jnp.zeros((128, 128), F32)
    for g in range(groups):
        first = jnp.broadcast_to(st_loc[g : g + 1, :], (128, 128)).T
        rows = pl.ds(g * 128, 128)
        cmask[rows, :] = jnp.where(first <= 0.0, one, zero).astype(BF16)
        tmask[:, rows] = jnp.where(lane + 128.0 * g >= tail_start, one, zero).astype(BF16)
        for k in range(2 * (g // 2) + 2):
            s = lane + 128.0 * k
            keep = s >= first
            if k == g:
                keep = keep & (lane <= sub)
            value = jnp.where(keep, one, zero) if k <= g else zero
            mask[rows, pl.ds(k * 128, 128)] = value.astype(BF16)

    pl.semaphore_wait(barrier, len(senders))

    ones_v = jnp.ones((tok, 128), BF16)

    def send(src, dst, s_sem, r_sem, dev):
        return pltpu.make_async_remote_copy(
            src_ref=src, dst_ref=dst, send_sem=s_sem, recv_sem=r_sem, device_id=dev, device_id_type=MESH
        )

    def send_w(p, u, src):
        return send(src, wr.at[p - 1, u], wr_s.at[p - 1, u], wr_r.at[p - 1, u], shard(1))

    def send_s(p, u, src):
        return send(src, sr.at[p, u], sr_s.at[p, u], sr_r.at[p, u], shard(-1))

    def send_y(p, u, src):
        return send(src, yr.at[p, u], yr_s.at[p, u], yr_r.at[p, u], shard(8))

    def send_t(p, u, src):
        dist = (1, 3, 5, 7)[p]
        return send(src, tr.at[p, u], tr_s.at[p, u], tr_r.at[p, u], shard(dist))

    @pl.loop(0, heads)
    def _(j):
        p = position(j)
        u = lax.rem(j // 2, 2)
        h = head_of(p, u)
        load(1, h).wait()
        kt = feature_map(kraw[h]).T
        kft[h] = kt
        load(2, h).wait()
        state = jnp.dot(
            kt * tmask[...],
            jnp.concatenate([vraw[h], ones_v], axis=1),
            preferred_element_type=F32,
        )
        tails[h, pl.ds(0, 128), :] = state[:, :128]
        tails[h, pl.ds(128, 8), :] = state[:, 128:].T[0:8, :]

        @pl.when((j < 4) & (p == 0))
        def _():
            send_w(1, u, tails.at[h]).start()

        @pl.when((j < 4) & (p == 3))
        def _():
            send_s(2, u, tails.at[h]).start()
            send_y(3, u, tails.at[h]).start()

    def row(r):
        return dl[pl.ds(r, 1), :]

    def gated(cond, x):
        return jnp.where(cond, x, 0.0)

    keep = lambda: row(8) == row(7)

    def handle_1(u):
        send_w(1, u, wo.at[0, u]).wait_recv()
        wo[0, u] = tails[head_of(1, u)] + gated(keep(), wr[0, u])
        send_w(2, u, wo.at[0, u]).start()
        send_s(2, u, so.at[2, u]).wait_recv()
        so[2, u] = gated(row(8) == row(9), tails[head_of(2, u)]) + sr[2, u]
        send_s(1, u, so.at[2, u]).start()
        send_y(2, u, so.at[2, u]).start()

    def handle_2(u):
        send_w(2, u, wo.at[1, u]).wait_recv()
        wo[1, u] = tails[head_of(2, u)] + gated(keep(), wr[1, u])
        send_w(3, u, wo.at[1, u]).start()
        send_s(1, u, so.at[1, u]).wait_recv()
        so[1, u] = gated(row(8) == row(10), tails[head_of(1, u)]) + sr[1, u]
        send_s(0, u, so.at[1, u]).start()
        tm[0, u] = so[2, u] + gated(row(7) == row(9), wr[1, u])
        send_t(1, u, tm.at[0, u]).start()
        tm[1, u] = so[1, u] + gated(row(7) == row(10), wr[0, u])
        send_t(2, u, tm.at[1, u]).start()
        send_y(1, u, so.at[1, u]).start()

    def handle_3(u):
        send_w(3, u, wo.at[2, u]).wait_recv()
        wo[2, u] = tails[head_of(3, u)] + gated(keep(), wr[2, u])
        send_t(0, u, wo.at[2, u]).start()
        send_s(0, u, so.at[0, u]).wait_recv()
        so[0, u] = gated(row(8) == row(11), tails[head_of(0, u)]) + sr[0, u]
        send_t(3, u, so.at[0, u]).start()
        send_y(0, u, so.at[0, u]).start()

    @pl.loop(0, heads)
    def _(h):
        for slot, handle in ((H1_SLOT, handle_1), (H2_SLOT, handle_2), (H3_SLOT, handle_3)):
            @pl.when(h == slot)
            def _():
                handle(0)
                handle(1)

        load(0, h).wait()
        qf[h] = feature_map(qraw[h])
        blk = 256
        for b in range(tok // blk):
            rows = pl.ds(b * blk, blk)
            width = (b + 1) * blk
            scores = jnp.dot(qf[h, rows, :], kft[h, :, pl.ds(0, width)], preferred_element_type=F32)
            weights = scores.astype(BF16) * mask[rows, pl.ds(0, width)]
            values = jnp.concatenate([vraw[h, pl.ds(0, width), :], ones_v[:width]], axis=1)
            nd[h, rows, :] = jnp.dot(weights, values, preferred_element_type=F32)

    sqacc[...] = jnp.zeros_like(sqacc)

    def store(h):
        return pltpu.make_async_copy(att.at[h], col(att_hbm, h), out_sem.at[h])

    for p in (1, 2, 0, 3):
        for u in range(heads // 4):
            h = head_of(p, u)
            send_t(p, u, so.at[0, u]).wait_recv()
            send_y(p, u, so.at[0, u]).wait_recv()
            first = df[0:1, :]
            carried = gated(first == row(7 - p), tr[p, u]) + gated(first == row(3 - p), yr[p, u])
            if p:
                carried = carried + gated(first == row(7), wr[p - 1, u])
            norm = jnp.broadcast_to(carried[128:129, :], (128, 128)).T
            both = jnp.concatenate([carried[:128, :], norm], axis=1)
            high = both.astype(BF16)
            low = (both - high.astype(F32)).astype(BF16)
            right = jnp.concatenate([high, low], axis=0)

            @pl.loop(0, tok // 256)
            def _(b):
                rows = pl.ds(pl.multiple_of(b * 256, 256), 256)
                q = qf[h, rows, :] * cmask[rows, :]
                extra = jnp.dot(jnp.concatenate([q, q], axis=1), right, preferred_element_type=F32)
                total = nd[h, rows, :] + extra
                out = total[:, :128] / total[:, 128:]
                att[h, rows, :] = out
                sqacc[rows, :] += out * out

            store(h).start()

    for g in range(groups):
        sq[0, pl.ds(g, 1), :] = jnp.sum(sqacc[pl.ds(g * 128, 128), :].T, axis=0, keepdims=True)

    def send_sq(j):
        return send(sq.at[0], sq.at[j], sq_s.at[j - 1], sq_r.at[j - 1], peer(j))

    for j in range(1, n_head):
        send_sq(j).start()
    for j in range(1, n_head):
        send_sq(j).wait_recv()
    total = jnp.sum(sq[...], axis=0)
    scale = lax.rsqrt(total / n_feat + 1e-06)
    for g in range(groups):
        scale_ref[pl.ds(g * 128, 128), :] = jnp.broadcast_to(scale[g : g + 1, :], (128, 128)).T

    for j in range(1, n_head):
        send_sq(j).wait_send()
    for u in range(heads // 4):
        for p in (1, 2, 3):
            send_w(p, u, wo.at[0, u]).wait_send()
        for p in (0, 1, 2):
            send_s(p, u, so.at[0, u]).wait_send()
        for p in range(4):
            send_y(p, u, so.at[0, u]).wait_send()
            send_t(p, u, so.at[0, u]).wait_send()

    @pl.loop(0, heads)
    def _(h):
        store(h).wait()


def body(n_seq, n_head, query_act, key_act, value_act, norm_gain, doc_lengths):
    tok, width = query_act.shape
    heads = width // E
    two = heads // 4
    any_spec = pl.BlockSpec(memory_space=pl.ANY)
    dma = pltpu.SemaphoreType.DMA
    state = lambda n: pltpu.VMEM((n, two, ROWS, 128), F32)
    att, scale = pl.pallas_call(
        functools.partial(kernel, n_seq, n_head, n_head * width),
        out_shape=(
            jax.ShapeDtypeStruct((tok, width), F32),
            jax.ShapeDtypeStruct((tok, 128), F32),
        ),
        in_specs=[any_spec, any_spec, any_spec, pl.BlockSpec(memory_space=pltpu.SMEM)],
        out_specs=(any_spec, pl.BlockSpec(memory_space=pltpu.VMEM)),
        scratch_shapes=[
            pltpu.VMEM((heads, tok, E), BF16),
            pltpu.VMEM((heads, tok, E), BF16),
            pltpu.VMEM((heads, tok, E), BF16),
            pltpu.VMEM((heads, tok, E), BF16),
            pltpu.VMEM((heads, E, tok), BF16),
            pltpu.VMEM((heads, ROWS, 128), F32),
            pltpu.VMEM((heads, tok, 256), F32),
            pltpu.VMEM((heads, tok, E), F32),
            pltpu.VMEM((tok, 128), F32),
            pltpu.VMEM((tok, tok), BF16),
            pltpu.VMEM((tok, 128), BF16),
            pltpu.VMEM((128, tok), BF16),
            pltpu.VMEM((16, 128), jnp.int32),
            pltpu.VMEM((8, 128), jnp.int32),
            state(3), state(3), state(4), state(4),
            state(3), state(3), state(2),
            pltpu.VMEM((n_head, 8, 128), F32),
            dma((3, heads)), dma((heads,)),
            dma((3, two)), dma((3, two)), dma((3, two)), dma((3, two)),
            dma((4, two)), dma((4, two)), dma((4, two)), dma((4, two)),
            dma((n_head - 1,)), dma((n_head - 1,)),
        ],
        compiler_params=pltpu.CompilerParams(
            collective_id=1, has_side_effects=True, vmem_limit_bytes=48 * 1024 * 1024
        ),
        name="attend",
    )(query_act, key_act, value_act, doc_lengths)
    gain = norm_gain.astype(F32)[None, :]
    return (att * scale[:, 0:1] * gain).astype(BF16)


def solution(mesh):
    in_specs = (P("seq", "head"), P("seq", "head"), P("seq", "head"), P("head"), P())
    fn = functools.partial(body, mesh.shape["seq"], mesh.shape["head"])
    return jax.shard_map(fn, mesh=mesh, in_specs=in_specs, out_specs=P("seq", "head"), check_vma=False)
```

time: 301 us -> 64.5 us (0.21)
  the two profiles are of different devices: /device:TPU:249 before, /device:TPU:1 now
where the time goes in v1:
time: 64.5 us; the launch traced here: 64.3 us
  Pallas kernels  55.6 us (86%)
  other arithmetic  4.62 us (7%)
  local copies, waits for them, and re-layouts  4.04 us (6%)
    pallas_call x1, Pallas kernels, body(): pl.pallas_call(functools.partial(kernel, n_seq, n_head, n_head * width),...  55.6 us
    convert_element_type x1, other arithmetic, body(): return (att * scale[:, 0:1] * gain).astype(BF16)  3.93 us
    unnamed x6, local copies, waits for them, and re-layouts  3.84 us

profile of v1, /device:TPU:1, one launch (start us, length us, event | category | flops | bytes accessed | tf_op | source)
XLA Modules:
  0.0 64.3 jit_solution(12071140585670217429)
XLA Ops:
  0.0 0.7 %convert_element_type.6 = f32[1024]{0:T(1024)S(1)} convert(bf16[1024]{0:T(1024)(128)(2,1)} %param.8) | non-fusion elementwise | flops 1024 | bytes 6144 | tf_op jit(solution)/shard_map/convert_element_type | solution.py:322
  0.7 0.0 copy-start
  0.7 1.6 %copy-done = bf16[1024,1024]{1,0:T(8,128)(2,1)S(1)} copy-done((bf16[1024,1024]{1,0:T(8,128)(2,1)S(1)}, bf16[1024,1024]{1,0:T(8,128)(2,1)}, u32[]{:S(2)}) %copy-start) | copy-done | bytes 2097176
  2.3 0.0 copy-start.1
  2.3 1.6 %copy-done.1 = bf16[1024,1024]{1,0:T(8,128)(2,1)S(1)} copy-done((bf16[1024,1024]{1,0:T(8,128)(2,1)S(1)}, bf16[1024,1024]{1,0:T(8,128)(2,1)}, u32[]{:S(2)}) %copy-start.1) | copy-done | bytes 2097176
  3.9 0.0 copy-start.2
  3.9 0.7 %copy-done.2 = s32[64]{0:T(128)S(1)} copy-done((s32[64]{0:T(128)S(1)}, s32[64]{0:T(128)}, u32[]{:S(2)}) %copy-start.2) | copy-done | bytes 280
  4.5 55.6 %attend.1 = (f32[1024,1024]{1,0:T(8,128)}, f32[1024,128]{1,0:T(8,128)S(1)}) custom-call(bf16[1024,1024]{1,0:T(8,128)(2,1)S(1)} %copy-done, bf16[1024,1024]{1,0:T(8,128)(2,1)S(1)} %copy-done.1, bf16[1024,1024]{1,0:T(8,128)(2,1)} %v_hbm.1, s32[64]{0:T(128)S(1)} %copy-done.2), custom_call_target="tpu_custom_call" | custom-call | tf_op jit(solution)/shard_map/attend/pallas_call | solution.py:286
  60.1 0.2 slice_reduce_fusion
  60.4 3.9 %multiply_convert_fusion = bf16[1024,1024]{1,0:T(8,128)(2,1)} fusion(f32[1024,1024]{1,0:T(8,128)} %get-tuple-element.7, f32[1024]{0:T(1024)S(1)} %convert_element_type.6, f32[1024]{0:T(1024)S(1)} %slice_reduce_fusion), kind=kLoop, calls=%fused_computation | loop fusion | flops 3145728 | bytes 6299648 | tf_op jit(solution)/shard_map/convert_element_type | solution.py:323
Async XLA Ops:
  0.7 1.6 %copy-start = (bf16[1024,1024]{1,0:T(8,128)(2,1)S(1)}, bf16[1024,1024]{1,0:T(8,128)(2,1)}, u32[]{:S(2)}) copy-start(bf16[1024,1024]{1,0:T(8,128)(2,1)} %q_hbm.1) | copy-start | bytes 6291460
  2.3 1.6 %copy-start.1 = (bf16[1024,1024]{1,0:T(8,128)(2,1)S(1)}, bf16[1024,1024]{1,0:T(8,128)(2,1)}, u32[]{:S(2)}) copy-start(bf16[1024,1024]{1,0:T(8,128)(2,1)} %k_hbm.1) | copy-start | bytes 6291460
  3.9 0.7 %copy-start.2 = (s32[64]{0:T(128)S(1)}, s32[64]{0:T(128)}, u32[]{:S(2)}) copy-start(s32[64]{0:T(128)} %len_ref.1) | copy-start | bytes 772

commit v2 on v1

v2 whole, which is shorter than its diff:
```python
import functools

import jax
import jax.numpy as jnp
from jax import lax
from jax.experimental import pallas as pl
from jax.experimental.pallas import tpu as pltpu
from jax.sharding import PartitionSpec as P

E = 128
ROWS = 136
PARTS = ((0, 136),)
MESH = pl.DeviceIdType.MESH
F32 = jnp.float32
BF16 = jnp.bfloat16


def feature_map(x):
    x = x.astype(F32)
    return jnp.where(x > 0.0, x + 1.0, jnp.exp(x)).astype(BF16)


def kernel(
    n_seq, n_head, n_feat,
    q_hbm, k_hbm, v_hbm, gain_hbm, len_hbm,
    out_hbm,
    qraw, kraw, vraw, qf, kft, tails, nd, att, sqacc,
    mask, cmask, tmask, dl, df,
    len_ref, gain, out, wr, sr, xr, wo, so, xo, car, sq,
    in_sem, small_sem, out_sem,
    wr_s, wr_r, sr_s, sr_r, xr_s, xr_r, sq_s, sq_r,
):
    heads, tok, _ = qraw.shape
    groups = tok // 128
    i = lax.axis_index("seq")
    hd = lax.axis_index("head")

    def shard(d):
        return (lax.rem(i + d + n_seq, n_seq), hd)

    def peer(j):
        return (i, lax.rem(hd + j, n_head))

    def position(j):
        return jnp.where(j < 4, 3 * lax.rem(j, 2), 1 + lax.rem(j, 2))

    def head_of(p, u):
        return lax.rem(i - p + 4 * n_seq, 4) + 4 * u

    def col(ref, h):
        return ref.at[:, pl.ds(pl.multiple_of(h * E, E), E)]

    def load(which, h):
        src, dst = ((q_hbm, qraw), (k_hbm, kraw), (v_hbm, vraw))[which]
        return pltpu.make_async_copy(col(src, h), dst.at[h], in_sem.at[which, h])

    lengths = pltpu.make_async_copy(len_hbm, len_ref, small_sem.at[0])
    gains = pltpu.make_async_copy(gain_hbm, gain, small_sem.at[1])
    lengths.start()
    barrier = pltpu.get_barrier_semaphore()
    senders = [shard(d) for d in (-1, 1, -8, -7)]
    senders += [peer(j) for j in range(1, n_head)]
    for dev in senders:
        pl.semaphore_signal(barrier, inc=1, device_id=dev, device_id_type=MESH)

    @pl.loop(0, heads)
    def _(j):
        h = head_of(position(j), lax.rem(j // 2, 2))
        load(1, h).start()
        load(2, h).start()

    @pl.loop(0, heads)
    def _(h):
        load(0, h).start()

    gains.start()
    lengths.wait()

    base = i * tok
    lane8 = lax.broadcasted_iota(jnp.int32, (8, 128), 1)
    sub8 = lax.broadcasted_iota(jnp.int32, (8, 128), 0)
    sub16 = lax.broadcasted_iota(jnp.int32, (16, 128), 0)
    pos_tok = base + sub8 * 128 + lane8
    pos_last = (i - 7 + sub16) * tok - 1
    pos_first = jnp.zeros((8, 128), jnp.int32) + base
    st_tok = jnp.zeros((8, 128), jnp.int32)
    st_last = jnp.where(pos_last < 0, -1, 0)
    st_first = jnp.zeros((8, 128), jnp.int32)
    end = jnp.int32(0)
    for d in range(len_ref.shape[0]):
        end = end + len_ref[d]
        st_tok = jnp.where(pos_tok >= end, end, st_tok)
        st_last = jnp.where(pos_last >= end, end, st_last)
        st_first = jnp.where(pos_first >= end, end, st_first)
    dl[...] = st_last
    df[...] = st_first

    lane = lax.broadcasted_iota(jnp.int32, (128, 128), 1).astype(F32)
    sub = lax.broadcasted_iota(jnp.int32, (128, 128), 0).astype(F32)
    st_loc = (st_tok - base).astype(F32)
    tail_start = (st_last[8:9, :] - base).astype(F32)
    one, zero = jnp.ones((128, 128), F32), jnp.zeros((128, 128), F32)
    for g in range(groups):
        rows = pl.ds(g * 128, 128)
        tmask[:, rows] = jnp.where(lane + 128.0 * g >= tail_start, one, zero).astype(BF16)

    pl.semaphore_wait(barrier, len(senders))

    ones_v = jnp.ones((tok, 128), BF16)

    def send(src, dst, s_sem, r_sem, dev):
        return pltpu.make_async_remote_copy(
            src_ref=src, dst_ref=dst, send_sem=s_sem, recv_sem=r_sem, device_id=dev, device_id_type=MESH
        )

    def part(ref, c):
        return ref.at[pl.ds(*PARTS[c]), :]

    def send_w(p, u, c, src):
        w = (p - 1, u, c)
        return send(part(src, c), part(wr.at[p - 1, u], c), wr_s.at[w], wr_r.at[w], shard(1))

    def send_s(p, u, c, src):
        w = (p, u, c)
        return send(part(src, c), part(sr.at[p, u], c), sr_s.at[w], sr_r.at[w], shard(-1))

    def send_x(kind, u, c, src):
        dist = (7, -1, 1, 1, 8, 8)[kind]
        w = (kind, u, c)
        return send(part(src, c), part(xr.at[kind, u], c), xr_s.at[w], xr_r.at[w], shard(dist))

    splits = range(len(PARTS))

    @pl.loop(0, heads)
    def _(j):
        p = position(j)
        u = lax.rem(j // 2, 2)
        h = head_of(p, u)
        load(1, h).wait()
        kt = feature_map(kraw[h]).T
        kft[h] = kt
        load(2, h).wait()
        state = jnp.dot(
            kt * tmask[...],
            jnp.concatenate([vraw[h], ones_v], axis=1),
            preferred_element_type=F32,
        )
        tails[h, pl.ds(0, 128), :] = state[:, :128]
        tails[h, pl.ds(128, 8), :] = state[:, 128:].T[0:8, :]

        @pl.when((j < 4) & (p == 0))
        def _():
            for c in splits:
                send_w(1, u, c, tails.at[h]).start()

        @pl.when((j < 4) & (p == 3))
        def _():
            for c in splits:
                send_s(2, u, c, tails.at[h]).start()

    for g in range(groups):
        first = jnp.broadcast_to(st_loc[g : g + 1, :], (128, 128)).T
        rows = pl.ds(g * 128, 128)
        cmask[rows, :] = jnp.where(first <= 0.0, one, zero).astype(BF16)
        for k in range(2 * (g // 2) + 2):
            s = lane + 128.0 * k
            keep = s >= first
            if k == g:
                keep = keep & (lane <= sub)
            value = jnp.where(keep, one, zero) if k <= g else zero
            mask[rows, pl.ds(k * 128, 128)] = value.astype(BF16)

    def row(r):
        return dl[pl.ds(r, 1), :]

    def gated(cond, x):
        return jnp.where(cond, x, 0.0)

    first = df[0:1, :]

    def prefix(p, u, c):
        rows = pl.ds(*PARTS[c])
        send_w(p, u, c, wo.at[p - 1, u]).wait_recv()
        wo[p - 1, u, rows] = tails[head_of(p, u), rows] + gated(row(8) == row(7), wr[p - 1, u, rows])
        if p < 3:
            send_w(p + 1, u, c, wo.at[p - 1, u]).start()

    def suffix(p, u, c):
        rows = pl.ds(*PARTS[c])
        send_s(p, u, c, so.at[p, u]).wait_recv()
        so[p, u, rows] = gated(row(8) == row(11 - p), tails[head_of(p, u), rows]) + sr[p, u, rows]
        if p:
            send_s(p - 1, u, c, so.at[p, u]).start()
        else:
            send_x(0, u, c, so.at[0, u]).start()

    wrapped = lax.rem(i, n_seq // 4) == 0

    def step(p, u):
        @pl.when(wrapped)
        def _():
            for c in splits:
                suffix(3 - p, u, c)
                prefix(p, u, c)

        @pl.when(jnp.logical_not(wrapped))
        def _():
            for c in splits:
                prefix(p, u, c)
                suffix(3 - p, u, c)

    def handle_4(u):
        for c in splits:
            rows = pl.ds(*PARTS[c])
            send_x(0, u, c, so.at[0, u]).wait_recv()
            send_x(1, u, c, xr.at[0, u]).start()
            xo[0, u, rows] = wo[2, u, rows] + gated(row(8) == row(4), xr[0, u, rows])
            send_x(2, u, c, xo.at[0, u]).start()

    def handle_5(u):
        for c in splits:
            rows = pl.ds(*PARTS[c])
            send_x(2, u, c, xo.at[0, u]).wait_recv()
            carried = gated(first == row(7), xr[2, u, rows])
            car[0, u, rows] = carried
            xo[1, u, rows] = tails[head_of(0, u), rows] + gated(row(8) == first, carried)
            send_x(3, u, c, xo.at[1, u]).start()

    def last_3(u):
        for c in splits:
            send_x(4, u, c, so.at[0, u]).wait_recv()
        car[3, u] = (
            gated(first == row(7), wr[2, u])
            + gated(first == row(4), xr[0, u])
            + gated(first == row(0), xr[4, u])
        )

    def last_2(u):
        for c in splits:
            send_x(1, u, c, so.at[0, u]).wait_recv()
            send_x(5, u, c, so.at[0, u]).wait_recv()
        car[2, u] = (
            gated(first == row(7), wr[1, u])
            + gated(first == row(5), xr[1, u])
            + gated(first == row(1), xr[5, u])
        )

    def last_1(u):
        for c in splits:
            send_x(3, u, c, so.at[0, u]).wait_recv()
        car[1, u] = gated(first == row(7), xr[3, u])

    @pl.loop(0, heads)
    def _(h):
        for p in (1, 2, 3):
            @pl.when(h // 2 == p - 1)
            def _():
                step(p, lax.rem(h, 2))

        @pl.when((h == 1) | (h == 2))
        def _():
            for c in splits:
                send_x(4, h - 1, c, tails.at[head_of(3, h - 1)]).start()

        @pl.when((h == 3) | (h == 4))
        def _():
            for c in splits:
                send_x(5, h - 3, c, so.at[2, h - 3]).start()

        @pl.when(h // 2 == 3)
        def _():
            handle_4(lax.rem(h, 2))

        load(0, h).wait()
        qf[h] = feature_map(qraw[h])
        blk = 256
        for b in range(tok // blk):
            rows = pl.ds(b * blk, blk)
            width = (b + 1) * blk
            scores = jnp.dot(qf[h, rows, :], kft[h, :, pl.ds(0, width)], preferred_element_type=F32)
            weights = scores.astype(BF16) * mask[rows, pl.ds(0, width)]
            values = jnp.concatenate([vraw[h, pl.ds(0, width), :], ones_v[:width]], axis=1)
            nd[h, rows, :] = jnp.dot(weights, values, preferred_element_type=F32)

    sqacc[...] = jnp.zeros_like(sqacc)

    def finish(p, u):
        h = head_of(p, u)
        carried = car[p, u]
        norm = jnp.broadcast_to(carried[128:129, :], (128, 128)).T
        both = jnp.concatenate([carried[:128, :], norm], axis=1)
        high = both.astype(BF16)
        low = (both - high.astype(F32)).astype(BF16)
        right = jnp.concatenate([high, low], axis=0)

        for b in range(tok // 256):
            rows = pl.ds(b * 256, 256)
            q = qf[h, rows, :] * cmask[rows, :]
            extra = jnp.dot(jnp.concatenate([q, q], axis=1), right, preferred_element_type=F32)
            total = nd[h, rows, :] + extra
            result = total[:, :128] / total[:, 128:]
            att[h, rows, :] = result
            sqacc[rows, :] += result * result

    last_3(0)
    finish(3, 0)
    handle_5(0)
    last_3(1)
    finish(3, 1)
    handle_5(1)
    finish(0, 0)
    last_2(0)
    finish(2, 0)
    finish(0, 1)
    last_2(1)
    finish(2, 1)
    last_1(0)
    finish(1, 0)
    last_1(1)
    finish(1, 1)

    for g in range(groups):
        sq[0, pl.ds(g, 1), :] = jnp.sum(sqacc[pl.ds(g * 128, 128), :].T, axis=0, keepdims=True)

    def send_sq(j):
        return send(sq.at[0], sq.at[j], sq_s.at[j - 1], sq_r.at[j - 1], peer(j))

    for j in range(1, n_head):
        send_sq(j).start()
    for j in range(1, n_head):
        send_sq(j).wait_recv()
    total = jnp.sum(sq[...], axis=0)
    scale = lax.rsqrt(total / n_feat + 1e-06)
    gains.wait()

    def store(g):
        rows = pl.ds(g * 128, 128)
        return pltpu.make_async_copy(out.at[rows, :], out_hbm.at[rows, :], out_sem.at[g])

    for g in range(groups):
        rows = pl.ds(g * 128, 128)
        factor = jnp.broadcast_to(scale[g : g + 1, :], (128, 128)).T
        for h in range(heads):
            cols = pl.ds(h * E, E)
            weight = gain[cols].astype(F32)[None, :]
            out[rows, cols] = (att[h, rows, :] * factor * weight).astype(BF16)
        store(g).start()

    for j in range(1, n_head):
        send_sq(j).wait_send()
    for u in range(heads // 4):
        for c in splits:
            for p in (1, 2, 3):
                send_w(p, u, c, wo.at[0, u]).wait_send()
            for p in (0, 1, 2):
                send_s(p, u, c, so.at[0, u]).wait_send()
            for kind in range(6):
                send_x(kind, u, c, xo.at[0, u]).wait_send()
    for g in range(groups):
        store(g).wait()


def body(n_seq, n_head, query_act, key_act, value_act, norm_gain, doc_lengths):
    tok, width = query_act.shape
    heads = width // E
    two = heads // 4
    any_spec = pl.BlockSpec(memory_space=pl.ANY)
    dma = pltpu.SemaphoreType.DMA
    state = lambda n: pltpu.VMEM((n, two, ROWS, 128), F32)
    arrivals = lambda n: dma((n, two, len(PARTS)))
    return pl.pallas_call(
        functools.partial(kernel, n_seq, n_head, n_head * width),
        out_shape=jax.ShapeDtypeStruct((tok, width), BF16),
        in_specs=[any_spec] * 5,
        out_specs=any_spec,
        scratch_shapes=[
            pltpu.VMEM((heads, tok, E), BF16),
            pltpu.VMEM((heads, tok, E), BF16),
            pltpu.VMEM((heads, tok, E), BF16),
            pltpu.VMEM((heads, tok, E), BF16),
            pltpu.VMEM((heads, E, tok), BF16),
            pltpu.VMEM((heads, ROWS, 128), F32),
            pltpu.VMEM((heads, tok, 256), F32),
            pltpu.VMEM((heads, tok, E), F32),
            pltpu.VMEM((tok, 128), F32),
            pltpu.VMEM((tok, tok), BF16),
            pltpu.VMEM((tok, 128), BF16),
            pltpu.VMEM((128, tok), BF16),
            pltpu.VMEM((16, 128), jnp.int32),
            pltpu.VMEM((8, 128), jnp.int32),
            pltpu.SMEM(doc_lengths.shape, jnp.int32),
            pltpu.VMEM((width,), BF16),
            pltpu.VMEM((tok, width), BF16),
            state(3), state(3), state(6),
            state(3), state(3), state(2), state(4),
            pltpu.VMEM((n_head, 8, 128), F32),
            dma((3, heads)), dma((2,)), dma((tok // 128,)),
            arrivals(3), arrivals(3), arrivals(3), arrivals(3),
            arrivals(6), arrivals(6),
            dma((n_head - 1,)), dma((n_head - 1,)),
        ],
        compiler_params=pltpu.CompilerParams(
            collective_id=1, has_side_effects=True, vmem_limit_bytes=62 * 1024 * 1024
        ),
        name="attend",
    )(query_act, key_act, value_act, norm_gain, doc_lengths)


def solution(mesh):
    in_specs = (P("seq", "head"), P("seq", "head"), P("seq", "head"), P("head"), P())
    fn = functools.partial(body, mesh.shape["seq"], mesh.shape["head"])
    return jax.shard_map(fn, mesh=mesh, in_specs=in_specs, out_specs=P("seq", "head"), check_vma=False)
```

time: 64.5 us -> 48.1 us (0.75)
  Pallas kernels: 55.6 us -> 45 us
  other arithmetic: 4.62 us -> 0 us
  local copies, waits for them, and re-layouts: 4.04 us -> 3.08 us
    pallas_call x1, Pallas kernels: 55.6 us -> 45 us  [body(): pl.pallas_call(functools.partial(kernel, n_seq, n_head, n_head * width),...]
    convert_element_type x2 -> x0, other arithmetic: 4.62 us -> none  [the longest x1 3.93 us: body(): return (att * scale[:, 0:1] * gain).astype(BF16)]
    unnamed x6 -> x1, local copies, waits for them, and re-layouts: 3.84 us -> 3.08 us
where the time goes in v2:
time: 48.1 us; the launch traced here: 48 us
  Pallas kernels  45 us (94%)
  local copies, waits for them, and re-layouts  3.08 us (6%)
    pallas_call x1, Pallas kernels, body(): pl.pallas_call(functools.partial(kernel, n_seq, n_head, n_head * width),...  45 us
    unnamed x1, local copies, waits for them, and re-layouts  3.08 us

profile of v2, /device:TPU:1, one launch (start us, length us, event | category | flops | bytes accessed | tf_op | source)
XLA Modules:
  0.0 48.0 jit_solution(6801177252721538923)
XLA Ops:
  0.0 45.0 %attend.1 = bf16[1024,1024]{1,0:T(8,128)(2,1)} custom-call(bf16[1024,1024]{1,0:T(8,128)(2,1)} %q_hbm.1, bf16[1024,1024]{1,0:T(8,128)(2,1)} %k_hbm.1, bf16[1024,1024]{1,0:T(8,128)(2,1)} %v_hbm.1, bf16[1024]{0:T(1024)(128)(2,1)} %gain_hbm.1, s32[64]{0:T(128)} %len_hbm.1), custom_call_target="tpu_custom_call" | custom-call | tf_op jit(solution)/shard_map/attend/pallas_call | solution.py:371
  45.0 3.1 %copy.7 = bf16[1024,1024]{1,0:T(8,128)(2,1)} copy(bf16[1024,1024]{1,0:T(8,128)(2,1)} %attend.1) | data formatting | bytes 4194304

commit v3 on v2

--- a/solution.py
+++ b/solution.py
@@ -10,6 +10,7 @@
 E = 128
 ROWS = 136
 PARTS = ((0, 136),)
+SLOTS = ((0, 0, 0), (1, 1, 0), (3, 0, 1), (4, 1, 1), (6, 0, 2), (7, 1, 2))
 MESH = pl.DeviceIdType.MESH
 F32 = jnp.float32
 BF16 = jnp.bfloat16
@@ -23,18 +24,21 @@
 def kernel(
     n_seq, n_head, n_feat,
     q_hbm, k_hbm, v_hbm, gain_hbm, len_hbm,
-    out_hbm,
+    out,
     qraw, kraw, vraw, qf, kft, tails, nd, att, sqacc,
     mask, cmask, tmask, dl, df,
-    len_ref, gain, out, wr, sr, xr, wo, so, xo, car, sq,
-    in_sem, small_sem, out_sem,
-    wr_s, wr_r, sr_s, sr_r, xr_s, xr_r, sq_s, sq_r,
+    len_ref, gain, wr, sr, xr, wo, so, xo, car, sq,
+    in_sem, small_sem,
+    rl, rl_s, rl_r, wr_s, wr_r, sr_s, sr_r, xr_s, xr_r, sq_s, sq_r,
 ):
     heads, tok, _ = qraw.shape
     groups = tok // 128
     i = lax.axis_index("seq")
     hd = lax.axis_index("head")
 
+    wrapped = lax.rem(i, n_seq // 4) == 0
+    over = jnp.where(wrapped, -8, 8)
+
     def shard(d):
         return (lax.rem(i + d + n_seq, n_seq), hd)
 
@@ -58,7 +62,7 @@
     gains = pltpu.make_async_copy(gain_hbm, gain, small_sem.at[1])
     lengths.start()
     barrier = pltpu.get_barrier_semaphore()
-    senders = [shard(d) for d in (-1, 1, -8, -7)]
+    senders = [shard(d) for d in (-1, 1, -over, -7)]
     senders += [peer(j) for j in range(1, n_head)]
     for dev in senders:
         pl.semaphore_signal(barrier, inc=1, device_id=dev, device_id_type=MESH)
@@ -125,11 +129,27 @@
         return send(part(src, c), part(sr.at[p, u], c), sr_s.at[w], sr_r.at[w], shard(-1))
 
     def send_x(kind, u, c, src):
-        dist = (7, -1, 1, 1, 8, 8)[kind]
+        dist = (7, -1, 1, 1, over, over)[kind]
         w = (kind, u, c)
         return send(part(src, c), part(xr.at[kind, u], c), xr_s.at[w], xr_r.at[w], shard(dist))
 
     splits = range(len(PARTS))
+
+    def send_relay(stage, kind, u, c, src):
+        w = (stage, kind, u, c)
+        return send(part(src, c), part(rl.at[stage, kind, u], c), rl_s.at[w], rl_r.at[w], shard(over))
+
+    def suffix_over(stage, kind, u, here):
+        own = tails.at[head_of(3, u)] if kind == 0 else so.at[2, u]
+        for c in splits:
+            if not here:
+                send_x(4 + kind, u, c, own).start()
+            elif stage == 0:
+                send_relay(0, kind, u, c, own).start()
+            else:
+                send_relay(stage - 1, kind, u, c, own).wait_recv()
+                src = rl.at[stage - 1, kind, u]
+                (send_relay(1, kind, u, c, src) if stage == 1 else send_x(4 + kind, u, c, src)).start()
 
     @pl.loop(0, heads)
     def _(j):
@@ -194,8 +214,6 @@
         else:
             send_x(0, u, c, so.at[0, u]).start()
 
-    wrapped = lax.rem(i, n_seq // 4) == 0
-
     def step(p, u):
         @pl.when(wrapped)
         def _():
@@ -203,7 +221,7 @@
                 suffix(3 - p, u, c)
                 prefix(p, u, c)
 
-        @pl.when(jnp.logical_not(wrapped))
+        @pl.when(lax.rem(i, n_seq // 4) != 0)
         def _():
             for c in splits:
                 prefix(p, u, c)
@@ -257,15 +275,18 @@
             def _():
                 step(p, lax.rem(h, 2))
 
-        @pl.when((h == 1) | (h == 2))
-        def _():
-            for c in splits:
-                send_x(4, h - 1, c, tails.at[head_of(3, h - 1)]).start()
-
-        @pl.when((h == 3) | (h == 4))
-        def _():
-            for c in splits:
-                send_x(5, h - 3, c, so.at[2, h - 3]).start()
+        v = lax.rem(h, 2)
+        for slot, kind, stage in SLOTS:
+            @pl.when((h == slot) & (lax.rem(i, n_seq // 4) == 0))
+            def _():
+                for u in range(2):
+                    suffix_over(stage, kind, u, True)
+
+            if stage == 0:
+                @pl.when((h == slot) & (lax.rem(i, n_seq // 4) != 0))
+                def _():
+                    for u in range(2):
+                        suffix_over(stage, kind, u, False)
 
         @pl.when(h // 2 == 3)
         def _():
@@ -333,10 +354,6 @@
     scale = lax.rsqrt(total / n_feat + 1e-06)
     gains.wait()
 
-    def store(g):
-        rows = pl.ds(g * 128, 128)
-        return pltpu.make_async_copy(out.at[rows, :], out_hbm.at[rows, :], out_sem.at[g])
-
     for g in range(groups):
         rows = pl.ds(g * 128, 128)
         factor = jnp.broadcast_to(scale[g : g + 1, :], (128, 128)).T
@@ -344,10 +361,17 @@
             cols = pl.ds(h * E, E)
             weight = gain[cols].astype(F32)[None, :]
             out[rows, cols] = (att[h, rows, :] * factor * weight).astype(BF16)
-        store(g).start()
 
     for j in range(1, n_head):
         send_sq(j).wait_send()
+    @pl.when(wrapped)
+    def _():
+        for u in range(heads // 4):
+            for c in splits:
+                for stage in (0, 1):
+                    for kind in (0, 1):
+                        send_relay(stage, kind, u, c, xo.at[0, u]).wait_send()
+
     for u in range(heads // 4):
         for c in splits:
             for p in (1, 2, 3):
@@ -356,8 +380,6 @@
                 send_s(p, u, c, so.at[0, u]).wait_send()
             for kind in range(6):
                 send_x(kind, u, c, xo.at[0, u]).wait_send()
-    for g in range(groups):
-        store(g).wait()
 
 
 def body(n_seq, n_head, query_act, key_act, value_act, norm_gain, doc_lengths):
@@ -370,9 +392,9 @@
     arrivals = lambda n: dma((n, two, len(PARTS)))
     return pl.pallas_call(
         functools.partial(kernel, n_seq, n_head, n_head * width),
-        out_shape=jax.ShapeDtypeStruct((tok, width), BF16),
+        out_shape=pltpu.VMEM((tok, width), BF16),
         in_specs=[any_spec] * 5,
-        out_specs=any_spec,
+        out_specs=pl.BlockSpec(memory_space=pltpu.VMEM),
         scratch_shapes=[
             pltpu.VMEM((heads, tok, E), BF16),
             pltpu.VMEM((heads, tok, E), BF16),
@@ -390,17 +412,18 @@
             pltpu.VMEM((8, 128), jnp.int32),
             pltpu.SMEM(doc_lengths.shape, jnp.int32),
             pltpu.VMEM((width,), BF16),
-            pltpu.VMEM((tok, width), BF16),
             state(3), state(3), state(6),
             state(3), state(3), state(2), state(4),
             pltpu.VMEM((n_head, 8, 128), F32),
-            dma((3, heads)), dma((2,)), dma((tok // 128,)),
+            dma((3, heads)), dma((2,)),
+            pltpu.VMEM((2, 2, two, ROWS, 128), F32),
+            dma((2, 2, two, len(PARTS))), dma((2, 2, two, len(PARTS))),
             arrivals(3), arrivals(3), arrivals(3), arrivals(3),
             arrivals(6), arrivals(6),
             dma((n_head - 1,)), dma((n_head - 1,)),
         ],
         compiler_params=pltpu.CompilerParams(
-            collective_id=1, has_side_effects=True, vmem_limit_bytes=62 * 1024 * 1024
+            collective_id=1, has_side_effects=True, vmem_limit_bytes=56 * 1024 * 1024
         ),
         name="attend",
     )(query_act, key_act, value_act, norm_gain, doc_lengths)

time: 48.1 us -> 44 us (0.915)
  Pallas kernels: 45 us -> 42.6 us
  local copies, waits for them, and re-layouts: 3.08 us -> 1.32 us
    pallas_call x1, Pallas kernels: 45 us -> 42.6 us  [body(): pl.pallas_call(functools.partial(kernel, n_seq, n_head, n_head * width),...]
    unnamed x1, local copies, waits for them, and re-layouts: 3.08 us -> 1.32 us
where the time goes in v3:
time: 44 us
  Pallas kernels  42.6 us (97%)
  local copies, waits for them, and re-layouts  1.32 us (3%)
    pallas_call x1, Pallas kernels, body(): pl.pallas_call(functools.partial(kernel, n_seq, n_head, n_head * width),...  42.6 us
    unnamed x1, local copies, waits for them, and re-layouts  1.32 us

profile of v3, /device:TPU:1, one launch (start us, length us, event | category | flops | bytes accessed | tf_op | source)
XLA Modules:
  0.0 44.0 jit_solution(11744458506014554567)
XLA Ops:
  0.0 42.6 %attend.1 = bf16[1024,1024]{1,0:T(8,128)(2,1)S(1)} custom-call(bf16[1024,1024]{1,0:T(8,128)(2,1)} %q_hbm.1, bf16[1024,1024]{1,0:T(8,128)(2,1)} %k_hbm.1, bf16[1024,1024]{1,0:T(8,128)(2,1)} %v_hbm.1, bf16[1024]{0:T(1024)(128)(2,1)} %gain_hbm.1, s32[64]{0:T(128)} %len_hbm.1), custom_call_target="tpu_custom_call" | custom-call | tf_op jit(solution)/shard_map/attend/pallas_call | solution.py:393
  42.6 1.3 %copy.7 = bf16[1024,1024]{1,0:T(8,128)(2,1)} copy(bf16[1024,1024]{1,0:T(8,128)(2,1)S(1)} %attend.1) | data formatting | bytes 4194304

commit v4 on v3

--- a/solution.py
+++ b/solution.py
@@ -9,7 +9,8 @@
 
 E = 128
 ROWS = 136
-PARTS = ((0, 136),)
+PARTS = ((0, 129),)
+SENT = 129
 SLOTS = ((0, 0, 0), (1, 1, 0), (3, 0, 1), (4, 1, 1), (6, 0, 2), (7, 1, 2))
 MESH = pl.DeviceIdType.MESH
 F32 = jnp.float32
@@ -36,7 +37,9 @@
     i = lax.axis_index("seq")
     hd = lax.axis_index("head")
 
-    wrapped = lax.rem(i, n_seq // 4) == 0
+    n_z = 8
+    z = lax.rem(i, n_z)
+    wrapped = z == 0
     over = jnp.where(wrapped, -8, 8)
 
     def shard(d):
@@ -66,6 +69,10 @@
     senders += [peer(j) for j in range(1, n_head)]
     for dev in senders:
         pl.semaphore_signal(barrier, inc=1, device_id=dev, device_id_type=MESH)
+
+    @pl.when(z == 1)
+    def _():
+        pl.semaphore_signal(barrier, inc=1, device_id=shard(-2), device_id_type=MESH)
 
     @pl.loop(0, heads)
     def _(j):
@@ -108,7 +115,7 @@
         rows = pl.ds(g * 128, 128)
         tmask[:, rows] = jnp.where(lane + 128.0 * g >= tail_start, one, zero).astype(BF16)
 
-    pl.semaphore_wait(barrier, len(senders))
+    pl.semaphore_wait(barrier, len(senders) + jnp.where(z == n_z - 1, 1, 0))
 
     ones_v = jnp.ones((tok, 128), BF16)
 
@@ -129,7 +136,7 @@
         return send(part(src, c), part(sr.at[p, u], c), sr_s.at[w], sr_r.at[w], shard(-1))
 
     def send_x(kind, u, c, src):
-        dist = (7, -1, 1, 1, over, over)[kind]
+        dist = (7, -1, 1, 1, over, over, 8, 2)[kind]
         w = (kind, u, c)
         return send(part(src, c), part(xr.at[kind, u], c), xr_s.at[w], xr_r.at[w], shard(dist))
 
@@ -204,6 +211,10 @@
         wo[p - 1, u, rows] = tails[head_of(p, u), rows] + gated(row(8) == row(7), wr[p - 1, u, rows])
         if p < 3:
             send_w(p + 1, u, c, wo.at[p - 1, u]).start()
+        else:
+            @pl.when(z != n_z - 1)
+            def _():
+                send_x(2, u, c, wo.at[2, u]).start()
 
     def suffix(p, u, c):
         rows = pl.ds(*PARTS[c])
@@ -214,83 +225,143 @@
         else:
             send_x(0, u, c, so.at[0, u]).start()
 
-    def step(p, u):
-        @pl.when(wrapped)
-        def _():
-            for c in splits:
-                suffix(3 - p, u, c)
-                prefix(p, u, c)
-
-        @pl.when(lax.rem(i, n_seq // 4) != 0)
-        def _():
-            for c in splits:
-                prefix(p, u, c)
-                suffix(3 - p, u, c)
+            @pl.when(z != 0)
+            def _():
+                send_x(6, u, c, so.at[0, u]).start()
+
+    def prefixes(p, u):
+        for c in splits:
+            prefix(p, u, c)
+
+    def suffixes(p, u):
+        for c in splits:
+            suffix(p, u, c)
+
+    def both(p, u):
+        for c in splits:
+            prefix(p, u, c)
+            suffix(3 - p, u, c)
+
+    def steps(h):
+        v = lax.rem(h, 2)
+        first_z, last_z = z == 0, z == n_z - 1
+        for p in (1, 2, 3):
+            @pl.when(first_z & (h == 2 * p))
+            def _():
+                prefixes(p, 1)
+
+            @pl.when(last_z & (h == 2 * p))
+            def _():
+                suffixes(3 - p, 1)
+
+        for p in (1, 2, 3):
+            @pl.when((z != 0) & (z != n_z - 1) & (h // 2 == p - 1))
+            def _():
+                both(p, v)
+
+            @pl.when(first_z & (h // 2 == p - 1))
+            def _():
+                suffixes(3 - p, v)
+
+            @pl.when(last_z & (h // 2 == p - 1))
+            def _():
+                prefixes(p, v)
+
+        for p in (1, 2, 3):
+            @pl.when(first_z & (h == 2 * p - 1))
+            def _():
+                prefixes(p, 0)
+
+            @pl.when(last_z & (h == 2 * p - 1))
+            def _():
+                suffixes(3 - p, 0)
 
     def handle_4(u):
         for c in splits:
             rows = pl.ds(*PARTS[c])
             send_x(0, u, c, so.at[0, u]).wait_recv()
             send_x(1, u, c, xr.at[0, u]).start()
-            xo[0, u, rows] = wo[2, u, rows] + gated(row(8) == row(4), xr[0, u, rows])
-            send_x(2, u, c, xo.at[0, u]).start()
-
-    def handle_5(u):
+
+            @pl.when(z == n_z - 1)
+            def _():
+                xo[0, u, rows] = wo[2, u, rows] + gated(row(8) == row(4), xr[0, u, rows])
+                send_x(2, u, c, xo.at[0, u]).start()
+                send_x(7, u, c, xo.at[0, u]).start()
+
+    def handle_5(u, here):
         for c in splits:
             rows = pl.ds(*PARTS[c])
             send_x(2, u, c, xo.at[0, u]).wait_recv()
             carried = gated(first == row(7), xr[2, u, rows])
+            if not here:
+                send_x(6, u, c, so.at[0, u]).wait_recv()
+                carried = carried + gated(first == row(3), xr[6, u, rows])
             car[0, u, rows] = carried
-            xo[1, u, rows] = tails[head_of(0, u), rows] + gated(row(8) == first, carried)
-            send_x(3, u, c, xo.at[1, u]).start()
+            if not here:
+                xo[1, u, rows] = tails[head_of(0, u), rows] + gated(row(8) == first, carried)
+                send_x(3, u, c, xo.at[1, u]).start()
+
+    head_rows = pl.ds(0, SENT)
 
     def last_3(u):
         for c in splits:
             send_x(4, u, c, so.at[0, u]).wait_recv()
-        car[3, u] = (
-            gated(first == row(7), wr[2, u])
-            + gated(first == row(4), xr[0, u])
-            + gated(first == row(0), xr[4, u])
+        car[3, u, head_rows] = (
+            gated(first == row(7), wr[2, u, head_rows])
+            + gated(first == row(4), xr[0, u, head_rows])
+            + gated(first == row(0), xr[4, u, head_rows])
         )
 
     def last_2(u):
         for c in splits:
             send_x(1, u, c, so.at[0, u]).wait_recv()
             send_x(5, u, c, so.at[0, u]).wait_recv()
-        car[2, u] = (
-            gated(first == row(7), wr[1, u])
-            + gated(first == row(5), xr[1, u])
-            + gated(first == row(1), xr[5, u])
+        car[2, u, head_rows] = (
+            gated(first == row(7), wr[1, u, head_rows])
+            + gated(first == row(5), xr[1, u, head_rows])
+            + gated(first == row(1), xr[5, u, head_rows])
         )
 
     def last_1(u):
-        for c in splits:
-            send_x(3, u, c, so.at[0, u]).wait_recv()
-        car[1, u] = gated(first == row(7), xr[3, u])
+        @pl.when(z == 1)
+        def _():
+            for c in splits:
+                send_x(7, u, c, so.at[0, u]).wait_recv()
+            car[1, u] = gated(first == row(7), wr[0, u]) + gated(first == row(6), xr[7, u])
+
+        @pl.when(z != 1)
+        def _():
+            for c in splits:
+                send_x(3, u, c, so.at[0, u]).wait_recv()
+            car[1, u] = gated(first == row(7), xr[3, u])
 
     @pl.loop(0, heads)
     def _(h):
-        for p in (1, 2, 3):
-            @pl.when(h // 2 == p - 1)
-            def _():
-                step(p, lax.rem(h, 2))
-
+        steps(h)
         v = lax.rem(h, 2)
         for slot, kind, stage in SLOTS:
-            @pl.when((h == slot) & (lax.rem(i, n_seq // 4) == 0))
+            @pl.when((h == slot) & (z == 0))
             def _():
                 for u in range(2):
                     suffix_over(stage, kind, u, True)
 
             if stage == 0:
-                @pl.when((h == slot) & (lax.rem(i, n_seq // 4) != 0))
+                @pl.when((h == slot + kind) & (z != 0))
                 def _():
                     for u in range(2):
                         suffix_over(stage, kind, u, False)
 
-        @pl.when(h // 2 == 3)
-        def _():
-            handle_4(lax.rem(h, 2))
+        @pl.when((h // 2 == 3) & ((z == 0) | (z == n_z - 1)))
+        def _():
+            handle_4(v)
+
+        @pl.when((h // 2 == 3) & (z != 0))
+        def _():
+            handle_5(v, False)
+
+        @pl.when((h // 2 == 3) & (z != 0) & (z != n_z - 1))
+        def _():
+            handle_4(v)
 
         load(0, h).wait()
         qf[h] = feature_map(qraw[h])
@@ -323,20 +394,25 @@
             att[h, rows, :] = result
             sqacc[rows, :] += result * result
 
+    def late(u):
+        @pl.when(z == 0)
+        def _():
+            handle_5(u, True)
+
     last_3(0)
     finish(3, 0)
-    handle_5(0)
+    late(0)
     last_3(1)
     finish(3, 1)
-    handle_5(1)
+    late(1)
     finish(0, 0)
+    finish(0, 1)
     last_2(0)
     finish(2, 0)
-    finish(0, 1)
+    last_1(0)
+    finish(1, 0)
     last_2(1)
     finish(2, 1)
-    last_1(0)
-    finish(1, 0)
     last_1(1)
     finish(1, 1)
 
@@ -378,8 +454,17 @@
                 send_w(p, u, c, wo.at[0, u]).wait_send()
             for p in (0, 1, 2):
                 send_s(p, u, c, so.at[0, u]).wait_send()
-            for kind in range(6):
+            for kind in (0, 1, 2, 4, 5):
                 send_x(kind, u, c, xo.at[0, u]).wait_send()
+
+            @pl.when(z != 0)
+            def _():
+                send_x(3, u, c, xo.at[0, u]).wait_send()
+                send_x(6, u, c, xo.at[0, u]).wait_send()
+
+            @pl.when(z == n_z - 1)
+            def _():
+                send_x(7, u, c, xo.at[0, u]).wait_send()
 
 
 def body(n_seq, n_head, query_act, key_act, value_act, norm_gain, doc_lengths):
@@ -412,14 +497,14 @@
             pltpu.VMEM((8, 128), jnp.int32),
             pltpu.SMEM(doc_lengths.shape, jnp.int32),
             pltpu.VMEM((width,), BF16),
-            state(3), state(3), state(6),
+            state(3), state(3), state(8),
             state(3), state(3), state(2), state(4),
             pltpu.VMEM((n_head, 8, 128), F32),
             dma((3, heads)), dma((2,)),
             pltpu.VMEM((2, 2, two, ROWS, 128), F32),
             dma((2, 2, two, len(PARTS))), dma((2, 2, two, len(PARTS))),
             arrivals(3), arrivals(3), arrivals(3), arrivals(3),
-            arrivals(6), arrivals(6),
+            arrivals(8), arrivals(8),
             dma((n_head - 1,)), dma((n_head - 1,)),
         ],
         compiler_params=pltpu.CompilerParams(

time: 44 us -> 42.9 us (0.975)
  Pallas kernels: 42.6 us -> 41.5 us
    pallas_call x1, Pallas kernels: 42.6 us -> 41.5 us  [body(): pl.pallas_call(functools.partial(kernel, n_seq, n_head, n_head * width),...]
where the time goes in v4:
time: 42.9 us; the launch traced here: 42.8 us
  Pallas kernels  41.5 us (97%)
  local copies, waits for them, and re-layouts  1.32 us (3%)
    pallas_call x1, Pallas kernels, body(): pl.pallas_call(functools.partial(kernel, n_seq, n_head, n_head * width),...  41.5 us
    unnamed x1, local copies, waits for them, and re-layouts  1.32 us

profile of v4, /device:TPU:1, one launch (start us, length us, event | category | flops | bytes accessed | tf_op | source)
XLA Modules:
  0.0 42.8 jit_solution(1357234501077527974)
XLA Ops:
  0.0 41.5 %attend.1 = bf16[1024,1024]{1,0:T(8,128)(2,1)S(1)} custom-call(bf16[1024,1024]{1,0:T(8,128)(2,1)} %q_hbm.1, bf16[1024,1024]{1,0:T(8,128)(2,1)} %k_hbm.1, bf16[1024,1024]{1,0:T(8,128)(2,1)} %v_hbm.1, bf16[1024]{0:T(1024)(128)(2,1)} %gain_hbm.1, s32[64]{0:T(128)} %len_hbm.1), custom_call_target="tpu_custom_call" | custom-call | tf_op jit(solution)/shard_map/attend/pallas_call | solution.py:478
  41.5 1.3 %copy.7 = bf16[1024,1024]{1,0:T(8,128)(2,1)} copy(bf16[1024,1024]{1,0:T(8,128)(2,1)S(1)} %attend.1) | data formatting | bytes 4194304

commit v5 on v4

--- a/solution.py
+++ b/solution.py
@@ -11,7 +11,8 @@
 ROWS = 136
 PARTS = ((0, 129),)
 SENT = 129
-SLOTS = ((0, 0, 0), (1, 1, 0), (3, 0, 1), (4, 1, 1), (6, 0, 2), (7, 1, 2))
+DIRECT = (1,)
+SLOTS = ((3, 0, 1), (6, 0, 2))
 MESH = pl.DeviceIdType.MESH
 F32 = jnp.float32
 BF16 = jnp.bfloat16
@@ -40,19 +41,35 @@
     n_z = 8
     z = lax.rem(i, n_z)
     wrapped = z == 0
-    over = jnp.where(wrapped, -8, 8)
+    over, back = 'over', 'back'
+
+    near = {d: lax.rem(i + d + n_seq, n_seq) for d in (-8, -7, -2, -1, 1, 2, 7, 8)}
+    near[over] = jnp.where(wrapped, near[-8], near[8])
+    near[back] = jnp.where(wrapped, near[8], near[-8])
+    classes = [lax.rem(i - p + 4 * n_seq, 4) for p in range(4)]
 
     def shard(d):
-        return (lax.rem(i + d + n_seq, n_seq), hd)
+        return (near[d], hd)
+
+    others = [lax.rem(hd + j, n_head) for j in range(n_head)]
 
     def peer(j):
-        return (i, lax.rem(hd + j, n_head))
+        return (i, others[j])
+
+    def odd(j):
+        return jnp.where((j == 1) | (j == 3) | (j == 5) | (j == 7), 1, 0)
 
     def position(j):
-        return jnp.where(j < 4, 3 * lax.rem(j, 2), 1 + lax.rem(j, 2))
+        return jnp.where(j < 4, 3 * odd(j), 1 + odd(j))
+
+    def second(j):
+        return jnp.where((j == 2) | (j == 3) | (j >= 6), 1, 0)
 
     def head_of(p, u):
-        return lax.rem(i - p + 4 * n_seq, 4) + 4 * u
+        if isinstance(p, int):
+            return classes[p] + 4 * u
+        own = jnp.where(p == 0, classes[0], jnp.where(p == 1, classes[1], jnp.where(p == 2, classes[2], classes[3])))
+        return own + 4 * u
 
     def col(ref, h):
         return ref.at[:, pl.ds(pl.multiple_of(h * E, E), E)]
@@ -65,18 +82,19 @@
     gains = pltpu.make_async_copy(gain_hbm, gain, small_sem.at[1])
     lengths.start()
     barrier = pltpu.get_barrier_semaphore()
-    senders = [shard(d) for d in (-1, 1, -over, -7)]
+    senders = [shard(d) for d in (-1, 1, back, -7)]
     senders += [peer(j) for j in range(1, n_head)]
     for dev in senders:
         pl.semaphore_signal(barrier, inc=1, device_id=dev, device_id_type=MESH)
 
-    @pl.when(z == 1)
-    def _():
-        pl.semaphore_signal(barrier, inc=1, device_id=shard(-2), device_id_type=MESH)
+    for cond, d in ((z == 0, -8), (z == 1, -2)):
+        @pl.when(cond)
+        def _():
+            pl.semaphore_signal(barrier, inc=1, device_id=shard(d), device_id_type=MESH)
 
     @pl.loop(0, heads)
     def _(j):
-        h = head_of(position(j), lax.rem(j // 2, 2))
+        h = head_of(position(j), second(j))
         load(1, h).start()
         load(2, h).start()
 
@@ -115,7 +133,7 @@
         rows = pl.ds(g * 128, 128)
         tmask[:, rows] = jnp.where(lane + 128.0 * g >= tail_start, one, zero).astype(BF16)
 
-    pl.semaphore_wait(barrier, len(senders) + jnp.where(z == n_z - 1, 1, 0))
+    pl.semaphore_wait(barrier, len(senders) + jnp.where((z == 0) | (z == n_z - 1), 1, 0))
 
     ones_v = jnp.ones((tok, 128), BF16)
 
@@ -136,7 +154,7 @@
         return send(part(src, c), part(sr.at[p, u], c), sr_s.at[w], sr_r.at[w], shard(-1))
 
     def send_x(kind, u, c, src):
-        dist = (7, -1, 1, 1, over, over, 8, 2)[kind]
+        dist = (7, -1, 1, 1, over, 8, 8, 2)[kind]
         w = (kind, u, c)
         return send(part(src, c), part(xr.at[kind, u], c), xr_s.at[w], xr_r.at[w], shard(dist))
 
@@ -146,22 +164,29 @@
         w = (stage, kind, u, c)
         return send(part(src, c), part(rl.at[stage, kind, u], c), rl_s.at[w], rl_r.at[w], shard(over))
 
-    def suffix_over(stage, kind, u, here):
-        own = tails.at[head_of(3, u)] if kind == 0 else so.at[2, u]
-        for c in splits:
-            if not here:
-                send_x(4 + kind, u, c, own).start()
-            elif stage == 0:
-                send_relay(0, kind, u, c, own).start()
-            else:
-                send_relay(stage - 1, kind, u, c, own).wait_recv()
-                src = rl.at[stage - 1, kind, u]
-                (send_relay(1, kind, u, c, src) if stage == 1 else send_x(4 + kind, u, c, src)).start()
+    def suffix_on(kind, u, c, source):
+        if kind in DIRECT:
+            send_x(4 + kind, u, c, source).start()
+            return
+
+        @pl.when(z != 0)
+        def _():
+            send_x(4 + kind, u, c, source).start()
+
+        @pl.when(z == 0)
+        def _():
+            send_relay(0, kind, u, c, source).start()
+
+    def relay(stage, kind, u):
+        for c in splits:
+            send_relay(stage - 1, kind, u, c, so.at[2, u]).wait_recv()
+            src = rl.at[stage - 1, kind, u]
+            (send_relay(1, kind, u, c, src) if stage == 1 else send_x(4 + kind, u, c, src)).start()
 
     @pl.loop(0, heads)
     def _(j):
         p = position(j)
-        u = lax.rem(j // 2, 2)
+        u = second(j)
         h = head_of(p, u)
         load(1, h).wait()
         kt = feature_map(kraw[h]).T
@@ -184,6 +209,7 @@
         def _():
             for c in splits:
                 send_s(2, u, c, tails.at[h]).start()
+                suffix_on(0, u, c, tails.at[h])
 
     for g in range(groups):
         first = jnp.broadcast_to(st_loc[g : g + 1, :], (128, 128)).T
@@ -222,6 +248,8 @@
         so[p, u, rows] = gated(row(8) == row(11 - p), tails[head_of(p, u), rows]) + sr[p, u, rows]
         if p:
             send_s(p - 1, u, c, so.at[p, u]).start()
+            if p == 2:
+                suffix_on(1, u, c, so.at[2, u])
         else:
             send_x(0, u, c, so.at[0, u]).start()
 
@@ -243,7 +271,7 @@
             suffix(3 - p, u, c)
 
     def steps(h):
-        v = lax.rem(h, 2)
+        v = odd(h)
         first_z, last_z = z == 0, z == n_z - 1
         for p in (1, 2, 3):
             @pl.when(first_z & (h == 2 * p))
@@ -255,15 +283,15 @@
                 suffixes(3 - p, 1)
 
         for p in (1, 2, 3):
-            @pl.when((z != 0) & (z != n_z - 1) & (h // 2 == p - 1))
+            @pl.when((z != 0) & (z != n_z - 1) & (h >= 2 * p - 2) & (h < 2 * p))
             def _():
                 both(p, v)
 
-            @pl.when(first_z & (h // 2 == p - 1))
+            @pl.when(first_z & (h >= 2 * p - 2) & (h < 2 * p))
             def _():
                 suffixes(3 - p, v)
 
-            @pl.when(last_z & (h // 2 == p - 1))
+            @pl.when(last_z & (h >= 2 * p - 2) & (h < 2 * p))
             def _():
                 prefixes(p, v)
 
@@ -338,28 +366,22 @@
     @pl.loop(0, heads)
     def _(h):
         steps(h)
-        v = lax.rem(h, 2)
+        v = odd(h)
         for slot, kind, stage in SLOTS:
             @pl.when((h == slot) & (z == 0))
             def _():
                 for u in range(2):
-                    suffix_over(stage, kind, u, True)
-
-            if stage == 0:
-                @pl.when((h == slot + kind) & (z != 0))
-                def _():
-                    for u in range(2):
-                        suffix_over(stage, kind, u, False)
-
-        @pl.when((h // 2 == 3) & ((z == 0) | (z == n_z - 1)))
+                    relay(stage, kind, u)
+
+        @pl.when((h >= 6) & ((z == 0) | (z == n_z - 1)))
         def _():
             handle_4(v)
 
-        @pl.when((h // 2 == 3) & (z != 0))
+        @pl.when((h >= 6) & (z != 0))
         def _():
             handle_5(v, False)
 
-        @pl.when((h // 2 == 3) & (z != 0) & (z != n_z - 1))
+        @pl.when((h >= 6) & (z != 0) & (z != n_z - 1))
         def _():
             handle_4(v)
 
@@ -445,7 +467,7 @@
         for u in range(heads // 4):
             for c in splits:
                 for stage in (0, 1):
-                    for kind in (0, 1):
+                    for kind in (0,):
                         send_relay(stage, kind, u, c, xo.at[0, u]).wait_send()
 
     for u in range(heads // 4):

time: 42.9 us -> 42.7 us (level)
  no operation moved by 1% of the time
where the time goes in v5:
time: 42.7 us; the launch traced here: 42.6 us
  Pallas kernels  41.3 us (97%)
  local copies, waits for them, and re-layouts  1.32 us (3%)
    pallas_call x1, Pallas kernels, body(): pl.pallas_call(functools.partial(kernel, n_seq, n_head, n_head * width),...  41.3 us
    unnamed x1, local copies, waits for them, and re-layouts  1.32 us

profile of v5, /device:TPU:1, one launch (start us, length us, event | category | flops | bytes accessed | tf_op | source)
XLA Modules:
  0.0 42.6 jit_solution(17605165708909766123)
XLA Ops:
  0.0 41.3 %attend.1 = bf16[1024,1024]{1,0:T(8,128)(2,1)S(1)} custom-call(bf16[1024,1024]{1,0:T(8,128)(2,1)} %q_hbm.1, bf16[1024,1024]{1,0:T(8,128)(2,1)} %k_hbm.1, bf16[1024,1024]{1,0:T(8,128)(2,1)} %v_hbm.1, bf16[1024]{0:T(1024)(128)(2,1)} %gain_hbm.1, s32[64]{0:T(128)} %len_hbm.1), custom_call_target="tpu_custom_call" | custom-call | tf_op jit(solution)/shard_map/attend/pallas_call | solution.py:500
  41.3 1.3 %copy.7 = bf16[1024,1024]{1,0:T(8,128)(2,1)} copy(bf16[1024,1024]{1,0:T(8,128)(2,1)S(1)} %attend.1) | data formatting | bytes 4194304

commit v6 on v5

--- a/solution.py
+++ b/solution.py
@@ -446,6 +446,32 @@
 
     for j in range(1, n_head):
         send_sq(j).start()
+    @pl.when(wrapped)
+    def _():
+        for u in range(heads // 4):
+            for c in splits:
+                for stage in (0, 1):
+                    for kind in (0,):
+                        send_relay(stage, kind, u, c, xo.at[0, u]).wait_send()
+
+    for u in range(heads // 4):
+        for c in splits:
+            for p in (1, 2, 3):
+                send_w(p, u, c, wo.at[0, u]).wait_send()
+            for p in (0, 1, 2):
+                send_s(p, u, c, so.at[0, u]).wait_send()
+            for kind in (0, 1, 2, 4, 5):
+                send_x(kind, u, c, xo.at[0, u]).wait_send()
+
+            @pl.when(z != 0)
+            def _():
+                send_x(3, u, c, xo.at[0, u]).wait_send()
+                send_x(6, u, c, xo.at[0, u]).wait_send()
+
+            @pl.when(z == n_z - 1)
+            def _():
+                send_x(7, u, c, xo.at[0, u]).wait_send()
+
     for j in range(1, n_head):
         send_sq(j).wait_recv()
     total = jnp.sum(sq[...], axis=0)
@@ -462,31 +488,6 @@
 
     for j in range(1, n_head):
         send_sq(j).wait_send()
-    @pl.when(wrapped)
-    def _():
-        for u in range(heads // 4):
-            for c in splits:
-                for stage in (0, 1):
-                    for kind in (0,):
-                        send_relay(stage, kind, u, c, xo.at[0, u]).wait_send()
-
-    for u in range(heads // 4):
-        for c in splits:
-            for p in (1, 2, 3):
-                send_w(p, u, c, wo.at[0, u]).wait_send()
-            for p in (0, 1, 2):
-                send_s(p, u, c, so.at[0, u]).wait_send()
-            for kind in (0, 1, 2, 4, 5):
-                send_x(kind, u, c, xo.at[0, u]).wait_send()
-
-            @pl.when(z != 0)
-            def _():
-                send_x(3, u, c, xo.at[0, u]).wait_send()
-                send_x(6, u, c, xo.at[0, u]).wait_send()
-
-            @pl.when(z == n_z - 1)
-            def _():
-                send_x(7, u, c, xo.at[0, u]).wait_send()
 
 
 def body(n_seq, n_head, query_act, key_act, value_act, norm_gain, doc_lengths):

time: 42.7 us -> 42.6 us (level)
  no operation moved by 1% of the time
where the time goes in v6:
time: 42.6 us
  Pallas kernels  41.2 us (97%)
  local copies, waits for them, and re-layouts  1.32 us (3%)
    pallas_call x1, Pallas kernels, body(): pl.pallas_call(functools.partial(kernel, n_seq, n_head, n_head * width),...  41.2 us
    unnamed x1, local copies, waits for them, and re-layouts  1.32 us

profile of v6, /device:TPU:1, one launch (start us, length us, event | category | flops | bytes accessed | tf_op | source)
XLA Modules:
  0.0 42.6 jit_solution(14503275487462295812)
XLA Ops:
  0.0 41.2 %attend.1 = bf16[1024,1024]{1,0:T(8,128)(2,1)S(1)} custom-call(bf16[1024,1024]{1,0:T(8,128)(2,1)} %q_hbm.1, bf16[1024,1024]{1,0:T(8,128)(2,1)} %k_hbm.1, bf16[1024,1024]{1,0:T(8,128)(2,1)} %v_hbm.1, bf16[1024]{0:T(1024)(128)(2,1)} %gain_hbm.1, s32[64]{0:T(128)} %len_hbm.1), custom_call_target="tpu_custom_call" | custom-call | tf_op jit(solution)/shard_map/attend/pallas_call | solution.py:501
  41.3 1.3 %copy.7 = bf16[1024,1024]{1,0:T(8,128)(2,1)} copy(bf16[1024,1024]{1,0:T(8,128)(2,1)S(1)} %attend.1) | data formatting | bytes 4194304
